TPU v7x, 128 devices: a whole 4x4x4 slice. The times are simulated.
128 devices in a mesh: col: 16 (over y, x), gpt: 8 (over z, core).
Axes of the slice: x: 4, y: 4, z: 4, core: 2. Of those that a mesh axis runs over, the one named last changes fastest.
Arguments:
- spectra: bfloat16 [64, 64, 33, 128], P('col', 'gpt'), may hold values from 0.0099487305 to 1
- cloud_top: int32 [64, 64], P('col', 'gpt'), may hold values from 0 to 63
- cloud_depth: int32 [64, 64], P('col', 'gpt'), may hold values from 1 to 64
- sun_order: int32 [64, 64], P('col', 'gpt'), may hold values from -1 to 31, as said below
- sunlit_cos: bfloat16 [64, 64], P('col', 'gpt'), may hold values from 0 to 1, as said below
- albedo: bfloat16 [64, 64, 14], P('col', 'gpt'), may hold values from 0.049804688 to 0.69921875
- temp: float32 [64, 64, 128], P('col', 'gpt'), may hold values from -6 to 6
- extinction: bfloat16 [33, 112], replicated, may hold values from 0.00029945374 to 0.0059814453
- scatter_albedo: float32 [33, 112], replicated, may hold values from 0.5 to 0.95
- gas_depth: float32 [112, 128], replicated, may hold values from 0.0005 to 0.01
- band_map: int32 [112], replicated, may hold values from 0 to 13, never falling along the last dimension, each value on 1 to 16 neighbouring positions
- solar_band: float32 [14], replicated, may hold values from 0.5 to 2
- heat_factor: float32 [128], replicated, may hold values from 1 to 10
Outputs:
- heating: float32 [64, 64, 128], P('col', 'gpt')
- temp_next: float32 [64, 64, 128], P('col', 'gpt')
Inputs may be any that keep to these rules, and one draw needn't show every extreme that they name: `sun_order`: every block of 4 x 8 columns of one device is wholly sunlit or wholly dark; a sunlit block carries each rank 0 to 31 once, a dark one -1 everywhere; in every row of such blocks along longitude exactly half are sunlit. `sunlit_cos`: positive exactly at the columns where sun_order is not -1, 0 at the others. `band_map`: never falls along the g-points; each band holds 1 to 2 * 112 // 14 g-points.
All inputs are finite; a program needn't handle non-finite values.
Results may differ from a plain program's by a relative error of at most 0.00056.
Values may be sent and summed in bfloat16 or wider, within the bound.
No kernel may reach another device: no remote copies, remote signals or barrier semaphores. Data moves between devices by JAX's collectives and lax.ppermute only.
A program may use at most 64 MiB of HBM per device.

v0:
```python
import jax
import jax.numpy as jnp
from jax import lax
from jax.sharding import PartitionSpec as P

ASYMMETRY = 0.85
DIFFUSION = 0.2


def padded_2(shard, sides, width):
    edges = {}
    for axis, dim in sides:
        size, length = (lax.axis_size(axis), shard.shape[dim])
        up = [(i, (i + 1) % size) for i in range(size)]
        last = lax.slice_in_dim(shard, length - width, length, axis=dim)
        leading = lax.slice_in_dim(shard, 0, width, axis=dim)
        edges[dim] = (
            lax.ppermute(last, axis, up),
            lax.ppermute(leading, axis, [(b, a) for a, b in up]),
        )
    done = []
    for _, dim in sides:
        low, high = edges[dim]
        around = [(width, width) if d in done else (0, 0) for d in range(shard.ndim)]
        shard = jnp.concatenate([jnp.pad(low, around), shard, jnp.pad(high, around)], axis=dim)
        done.append(dim)
    return shard


def mobius_join(earlier, following):
    upper_left = following[0] * earlier[0] + following[1] * earlier[2]
    upper_right = following[0] * earlier[1] + following[1] * earlier[3]
    lower_left = following[2] * earlier[0] + following[3] * earlier[2]
    lower_right = following[2] * earlier[1] + following[3] * earlier[3]
    scale_sum = (
        jnp.abs(upper_left) + jnp.abs(upper_right) + jnp.abs(lower_left) + jnp.abs(lower_right)
    )
    return (
        upper_left / scale_sum,
        upper_right / scale_sum,
        lower_left / scale_sum,
        lower_right / scale_sum,
    )


def two_stream(ext_total, cloud_sca):
    scat_ratio = cloud_sca / ext_total
    gamma_one = 2.0 - scat_ratio * (1.0 + ASYMMETRY)
    gamma_two = scat_ratio * (1.0 - ASYMMETRY)
    eigen_val = jnp.sqrt((2.0 - 2.0 * scat_ratio) * (2.0 - 2.0 * ASYMMETRY * scat_ratio))
    layer_decay = jnp.exp(-eigen_val * ext_total)
    decay_sq = layer_decay * layer_decay
    denom_sum = eigen_val + gamma_one + (eigen_val - gamma_one) * decay_sq
    reflect = gamma_two * (1.0 - decay_sq) / denom_sum
    transmit = 2.0 * eigen_val * layer_decay / denom_sum
    return (reflect, transmit)


def level_heating(ext_total, cloud_sca, surface, incoming):
    levels, rows, width = ext_total.shape
    ext_flat = ext_total.reshape(levels, rows * width)
    sca_flat = cloud_sca.reshape(levels, rows * width)
    surface_row = surface.reshape(1, rows * width)
    incoming_row = incoming.reshape(1, rows * width)
    reflect, transmit = two_stream(ext_flat, sca_flat)
    matrices = (transmit * transmit - reflect * reflect, reflect, -reflect, jnp.ones_like(reflect))
    flipped = tuple((member[::-1] for member in matrices))
    scanned = lax.associative_scan(mobius_join, flipped, axis=0)
    product = tuple((member[::-1] for member in scanned))
    reflect_top = (product[0] * surface_row + product[1]) / (product[2] * surface_row + product[3])
    reflect_below = jnp.concatenate([reflect_top[1:], surface_row], axis=0)
    factor = transmit / (1.0 - reflect * reflect_below)
    through = lax.associative_scan(jnp.multiply, factor, axis=0)
    above_flux = jnp.concatenate([jnp.ones_like(through[:1]), through[:-1]], axis=0)
    absorbed = incoming_row * (above_flux * (1.0 - reflect_top) - through * (1.0 - reflect_below))
    return jnp.sum(absorbed.reshape(levels, rows, width), axis=2)


def compute_optics(spec_rows, optic_table):
    optics = jnp.einsum("cbl,bk->ckl", spec_rows, optic_table, preferred_element_type=jnp.float32)
    return lax.optimization_barrier(optics.astype(jnp.bfloat16))


def radiate(cloud_opt, gas_part, surface, incoming):
    opt_wide = cloud_opt.astype(jnp.float32)
    ext_levels = jnp.transpose(opt_wide[:, 0], (2, 0, 1))
    sca_levels = jnp.transpose(opt_wide[:, 1], (2, 0, 1))
    ext_total = ext_levels + gas_part.T[:, None, :]
    return level_heating(ext_total, sca_levels, surface, incoming).T


def shards(
    spectra,
    cloud_top,
    cloud_depth,
    sun_order,
    sunlit_cos,
    albedo,
    temp,
    extinction,
    scatter_albedo,
    gas_depth,
    band_map,
    solar_band,
    heat_factor,
):
    padded = padded_2(temp, (("col", 0), ("gpt", 1)), 1)
    tile_lon, tile_lat, bin_count, levels = spectra.shape
    band_count = albedo.shape[2]
    tile_cols = tile_lon * tile_lat
    num_groups = lax.axis_size("gpt")
    gpoints = extinction.shape[1]
    group_width = gpoints // num_groups
    level_ids = jnp.arange(levels, dtype=jnp.int32)
    cloud_end = cloud_top + cloud_depth
    cloudy = (level_ids >= cloud_top[..., None]) & (level_ids < cloud_end[..., None])
    masked = (spectra * cloudy[:, :, None, :].astype(jnp.bfloat16)).reshape(
        tile_cols, bin_count, levels
    )
    scatter_table = (extinction.astype(jnp.float32) * scatter_albedo).astype(jnp.bfloat16)
    band_onehot = (band_map[:, None] == jnp.arange(band_count, dtype=jnp.int32)[None, :]).astype(
        jnp.float32
    )
    band_select = band_onehot.astype(jnp.bfloat16).T
    solar_g = jnp.dot(band_onehot, solar_band, precision=lax.Precision.HIGHEST)
    order_flat = sun_order.reshape(tile_cols)
    cos_flat = sunlit_cos.reshape(tile_cols)
    albedo_flat = albedo.reshape(tile_cols, band_count)

    def group_table(group_start):
        ext_part = lax.dynamic_slice_in_dim(extinction, group_start, group_width, 1)
        sca_part = lax.dynamic_slice_in_dim(scatter_table, group_start, group_width, 1)
        return jnp.concatenate([ext_part, sca_part], axis=1)

    surface_all = jnp.dot(albedo_flat, band_select, preferred_element_type=jnp.float32)
    incoming_all = cos_flat.astype(jnp.float32)[:, None] * solar_g[None, :]

    def add_group(group_id, running_sum):
        group_start = group_id * group_width
        cloud_opt = compute_optics(masked, group_table(group_start)).reshape(
            tile_cols, 2, group_width, levels
        )
        gas_part = lax.dynamic_slice_in_dim(gas_depth, group_start, group_width, 0)
        surface_part = lax.dynamic_slice_in_dim(surface_all, group_start, group_width, 1)
        incoming_part = lax.dynamic_slice_in_dim(incoming_all, group_start, group_width, 1)
        return running_sum + radiate(cloud_opt, gas_part, surface_part, incoming_part)

    summed = lax.fori_loop(0, num_groups, add_group, jnp.zeros((tile_cols, levels), jnp.float32))
    summed = summed * (order_flat >= 0).astype(jnp.float32)[:, None]
    heating = (summed * heat_factor[None, :]).reshape(tile_lon, tile_lat, levels)
    laplace = (
        padded[2:, 1:-1] + padded[:-2, 1:-1] + padded[1:-1, 2:] + padded[1:-1, :-2] - 4.0 * temp
    )
    temp_next = temp + DIFFUSION * laplace + heating
    return (heating, temp_next)


def solution(mesh):
    in_specs = (
        P("col", "gpt", None, None),
        P("col", "gpt"),
        P("col", "gpt"),
        P("col", "gpt"),
        P("col", "gpt"),
        P("col", "gpt", None),
        P("col", "gpt", None),
        P(),
        P(),
        P(),
        P(),
        P(),
        P(),
    )
    out_specs = (P("col", "gpt", None), P("col", "gpt", None))
    return jax.shard_map(shards, mesh=mesh, in_specs=in_specs, out_specs=out_specs, check_vma=False)
```

profile of v0, /device:TPU:1, one launch (start us, length us, event | category | flops | bytes accessed | tf_op | source)
XLA Modules:
  0.0 167.2 jit_solution(17012702900918101183)
XLA Ops:
  0.7 0.8 fusion.55
  1.5 1.4 collective-permute-start.2
  2.9 1.6 collective-permute-start.3
  4.5 0.7 fusion.56
  5.2 4.9 %collective-permute-start = (f32[1,8,128]{2,1,0:T(8,128)S(1)}, f32[1,8,128]{2,1,0:T(8,128)S(1)}, u32[]{:S(2)}, u32[]{:S(2)}) collective-permute-start(f32[1,8,128]{2,1,0:T(8,128)S(1)} %get-tuple-element.349), channel_id=1, source_target_pairs={{8,0},{16,8},{24,16},{32,24},{40,32},{48,40},{56,48},{64,56},{72,6... | collective-permute-start | bytes 12296 | tf_op jit(solution)/shard_map/ppermute | solution.py:19
  10.1 0.8 reshape.91
  10.9 0.7 add.1130
  11.6 0.8 fusion.25
  12.3 0.9 convolution_bitcast_fusion.1
  13.2 0.9 convolution_bitcast_fusion
  14.1 0.8 copy.188
  15.0 0.8 copy.186
  16.0 149.7 %while.14 = (s32[]{:T(128)}, f32[32,128]{1,0:T(8,128)S(1)}, f32[32,112]{1,0:T(8,128)S(1)}, bf16[33,112]{0,1:T(8,128)(2,1)S(1)}, bf16[33,112]{0,1:T(8,128)(2,1)S(...) while((s32[]{:T(128)}, f32[32,128]{1,0:T(8,128)S(1)}, ...), condition=%wide.region_2.3_spmd.clone, body=%wide.region_0.2_spmd.clone.sunk | while | flops 15025207 | bytes 50594164 | solution.py:148
  16.0 0.7 dynamic-slice_bitcast_fusion.2
  27.9 0.6 copy-done.2
  30.5 0.7 slice-done.4
  31.3 0.7 slice-done.3
  32.0 0.7 slice-done.2
  32.8 0.6 slice-done.1
  33.5 0.6 slice-done
  34.7 0.7 dynamic-slice_bitcast_fusion.2
  49.2 0.7 slice-done.4
  50.0 0.7 slice-done.3
  50.7 0.7 slice-done.2
  51.5 0.6 slice-done.1
  52.3 0.6 slice-done
  53.4 0.7 dynamic-slice_bitcast_fusion.2
  68.0 0.7 slice-done.4
  68.7 0.7 slice-done.3
  69.4 0.7 slice-done.2
  70.2 0.6 slice-done.1
  71.0 0.6 slice-done
  72.1 0.7 dynamic-slice_bitcast_fusion.2
  86.7 0.7 slice-done.4
  87.4 0.7 slice-done.3
  88.2 0.7 slice-done.2
  88.9 0.6 slice-done.1
  89.7 0.6 slice-done
  90.9 0.7 dynamic-slice_bitcast_fusion.2
  105.4 0.7 slice-done.4
  106.1 0.7 slice-done.3
  106.9 0.7 slice-done.2
  107.6 0.6 slice-done.1
  108.4 0.6 slice-done
  109.6 0.7 dynamic-slice_bitcast_fusion.2
  124.1 0.7 slice-done.4
  124.8 0.7 slice-done.3
  125.6 0.7 slice-done.2
  126.3 0.6 slice-done.1
  127.1 0.6 slice-done
  128.3 0.7 dynamic-slice_bitcast_fusion.2
  142.8 0.7 slice-done.4
  143.5 0.7 slice-done.3
  144.3 0.7 slice-done.2
  145.0 0.6 slice-done.1
  145.8 0.6 slice-done
  147.0 0.7 dynamic-slice_bitcast_fusion.2
  161.5 0.7 slice-done.4
  162.2 0.7 slice-done.3
  163.0 0.7 slice-done.2
  163.7 0.6 slice-done.1
  164.5 0.6 slice-done
  165.9 0.6 copy-done.9
  166.5 0.7 fusion.21
  (2591 shorter events, 103.7 us)
Async XLA Ops:
  0.6 12.6 %copy-start = (bf16[4,8,14]{2,1,0:T(8,128)(2,1)S(1)}, bf16[4,8,14]{2,1,0:T(8,128)(2,1)}, u32[]{:S(2)}) copy-start(bf16[4,8,14]{2,1,0:T(8,128)(2,1)} %param.20) | copy-start | bytes 2692
  0.6 15.1 %copy-start.6 = (bf16[4,8,33,128]{3,1,2,0:T(8,128)(2,1)S(1)}, bf16[4,8,33,128]{3,1,2,0:T(8,128)(2,1)}, u32[]{:S(2)}) copy-start(bf16[4,8,33,128]{3,1,2,0:T(8,128)(2,1)} %param.15) | copy-start | bytes 811012
  1.5 164.4 %collective-permute-start.2 = (f32[4,1,128]{2,1,0:T(1,128)S(1)}, f32[4,1,128]{2,1,0:T(1,128)S(1)}, u32[]{:S(2)}, u32[]{:S(2)}) collective-permute-start(f32[4,1,128]{2,1,0:T(1,128)S(1)} %get-tuple-element.347), channel_id=1, source_target_pairs={{1,0},{2,1},{3,2},{4,3},{5,4},{6,5},{7,6},{0,7},{9,8},{10,9},{11,1... | collective-permute-start | bytes 6152 | tf_op jit(solution)/shard_map/ppermute | solution.py:19
  2.9 163.0 %collective-permute-start.3 = (f32[4,1,128]{2,1,0:T(1,128)S(1)}, f32[4,1,128]{2,1,0:T(1,128)S(1)}, u32[]{:S(2)}, u32[]{:S(2)}) collective-permute-start(f32[4,1,128]{2,1,0:T(1,128)S(1)} %get-tuple-element.348), channel_id=1, source_target_pairs={{0,1},{1,2},{2,3},{3,4},{4,5},{5,6},{6,7},{7,0},{8,9},{9,10},{10,1... | collective-permute-start | bytes 6152 | tf_op jit(solution)/shard_map/ppermute | solution.py:18
  5.2 160.6 %collective-permute-start = (f32[1,8,128]{2,1,0:T(8,128)S(1)}, f32[1,8,128]{2,1,0:T(8,128)S(1)}, u32[]{:S(2)}, u32[]{:S(2)}) collective-permute-start(f32[1,8,128]{2,1,0:T(8,128)S(1)} %get-tuple-element.349), channel_id=1, source_target_pairs={{8,0},{16,8},{24,16},{32,24},{40,32},{48,40},{56,48},{64,56},{72,6... | collective-permute-start | bytes 12296 | tf_op jit(solution)/shard_map/ppermute | solution.py:19
  10.1 155.7 %collective-permute-start.1 = (f32[1,8,128]{2,1,0:T(8,128)S(1)}, f32[1,8,128]{2,1,0:T(8,128)S(1)}, u32[]{:S(2)}, u32[]{:S(2)}) collective-permute-start(f32[1,8,128]{2,1,0:T(8,128)S(1)} %get-tuple-element.350), channel_id=1, source_target_pairs={{0,8},{8,16},{16,24},{24,32},{32,40},{40,48},{48,56},{56,64},{64,7... | collective-permute-start | bytes 12296 | tf_op jit(solution)/shard_map/ppermute | solution.py:18
  16.0 149.7 %copy-start.8 = (s32[4,8]{1,0:T(4,128)S(1)}, s32[4,8]{1,0:T(4,128)}, u32[]{:S(2)}) copy-start(s32[4,8]{1,0:T(4,128)} %param.18) | copy-start | bytes 388
  16.0 149.8 %copy-start.7 = (f32[4,8,128]{2,1,0:T(8,128)S(1)}, f32[4,8,128]{2,1,0:T(8,128)}, u32[]{:S(2)}) copy-start(f32[4,8,128]{2,1,0:T(8,128)} %param.21) | copy-start | bytes 49156
  26.9 0.7 copy-start.1
  27.8 0.7 copy-start.2
  30.5 0.7 slice-start.4
  31.2 0.7 slice-start.3
  32.0 0.7 slice-start.2
  32.7 0.7 slice-start.1
  33.5 0.7 slice-start
  45.7 0.7 copy-start.1
  46.5 0.7 copy-start.2
  49.2 0.7 slice-start.4
  50.0 0.7 slice-start.3
  50.7 0.7 slice-start.2
  51.5 0.7 slice-start.1
  52.2 0.7 slice-start
  64.4 0.7 copy-start.1
  65.2 0.7 copy-start.2
  67.9 0.7 slice-start.4
  68.7 0.7 slice-start.3
  69.4 0.7 slice-start.2
  70.2 0.7 slice-start.1
  70.9 0.7 slice-start
  83.1 0.7 copy-start.1
  83.9 0.7 copy-start.2
  86.6 0.7 slice-start.4
  87.4 0.7 slice-start.3
  88.1 0.7 slice-start.2
  89.6 0.7 slice-start
  101.8 0.7 copy-start.1
  102.6 0.7 copy-start.2
  105.3 0.7 slice-start.4
  106.1 0.7 slice-start.3
  106.8 0.7 slice-start.2
  107.6 0.7 slice-start.1
  108.3 0.7 slice-start
  120.5 0.7 copy-start.1
  121.3 0.7 copy-start.2
  124.1 0.7 slice-start.4
  124.8 0.7 slice-start.3
  125.5 0.7 slice-start.2
  126.3 0.7 slice-start.1
  127.1 0.7 slice-start
  139.2 0.7 copy-start.1
  140.0 0.7 copy-start.2
  142.8 0.7 slice-start.4
  143.5 0.7 slice-start.3
  144.3 0.7 slice-start.2
  145.0 0.7 slice-start.1
  145.8 0.7 slice-start
  157.9 0.7 copy-start.1
  158.7 0.7 copy-start.2
  161.5 0.7 slice-start.4
  162.2 0.7 slice-start.3
  163.0 0.7 slice-start.2
  163.7 0.7 slice-start.1
  164.5 0.7 slice-start
  165.8 0.7 copy-start.9
  (25 other events, 15.3 us)
where the time goes:
time: 170 us; the launch traced here: 167 us
  local copies, waits for them, and re-layouts  114 us (67%)
  other arithmetic  26.5 us (16%)
  loops' own time  14.2 us (8%)
  starting transfers between devices  7.96 us (5%)
  matrix products  3.5 us (2%)
    slice x216, local copies, waits for them, and re-layouts, level_heating(): through = lax.associative_scan(jnp.multiply, factor, axis=0)  31.8 us
    slice x752, local copies, waits for them, and re-layouts, level_heating(): scanned = lax.associative_scan(mobius_join, flipped, axis=0)  28.6 us
    while x80, local copies, waits for them, and re-layouts  20.4 us
    another operation x1, loops' own time, shards(): lax.fori_loop(0, num_groups, add_group, jnp.zeros((tile_cols, levels), jn...  14.2 us
    pad x384, local copies, waits for them, and re-layouts, level_heating(): scanned = lax.associative_scan(mobius_join, flipped, axis=0)  6.66 us
    ppermute x2, starting transfers between devices, padded_2(): lax.ppermute(leading, axis, [(b, a) for a, b in up])  6.35 us
    transpose x8, local copies, waits for them, and re-layouts, radiate(): ext_total = ext_levels + gas_part.T[:, None, :]  5.75 us
    rev x32, local copies, waits for them, and re-layouts, level_heating(): product = tuple((member[::-1] for member in scanned))  4.46 us
  transfers between devices with their start and end apart: 4, of which 0 were waited for; matrix products, arithmetic and copies ran while one was open for 57% of the time, Pallas kernels for 0%

commit v1 on v0

v1 whole, which is shorter than its diff:
```python
import functools
import jax
import jax.numpy as jnp
from jax import lax
from jax.experimental import pallas as pl
from jax.experimental.pallas import tpu as pltpu
from jax.sharding import PartitionSpec as P

DIFFUSION = 0.2
CHUNK = 8


def column_of(row, size):
    spread = jnp.broadcast_to(row, (size, size))
    lane = lax.broadcasted_iota(jnp.int32, (size, size), 1)
    sublane = lax.broadcasted_iota(jnp.int32, (size, size), 0)
    return jnp.sum(jnp.where(lane == sublane, spread, jnp.zeros_like(spread)), axis=1, keepdims=True)


def radiation_kernel(
    spec_ref, top_ref, depth_ref, order_ref, cos_ref, albedo_ref, temp_ref,
    ext_ref, scat_ref, gas_ref, band_ref, solar_ref, factor_ref,
    heat_ref, base_ref,
    binned, rows_ref, optics, gas_levels, table, steps,
):
    lon, bins, lat, levels = spec_ref.shape
    gpoints = ext_ref.shape[1]
    bands = albedo_ref.shape[2]
    tall = binned.shape[0] // lat
    wide = 128
    block = CHUNK * lon * lat

    table[...] = jnp.zeros_like(table)
    ext = ext_ref[...]
    table[:bins, :gpoints] = ext
    table[:bins, wide : wide + gpoints] = (ext.astype(jnp.float32) * scat_ref[...]).astype(jnp.bfloat16)
    gas_levels[...] = jnp.zeros_like(gas_levels)
    gas_levels[:, :gpoints] = gas_ref[...].T

    onehot = (
        lax.broadcasted_iota(jnp.int32, (bands, gpoints), 0) == band_ref[...]
    ).astype(jnp.float32)
    solar_g = jnp.dot(
        solar_ref[...], onehot, precision=lax.Precision.HIGHEST, preferred_element_type=jnp.float32
    )

    level_lane = lax.broadcasted_iota(jnp.int32, (lat, levels), 1)
    top_all = top_ref[...].astype(jnp.float32)
    end_all = top_all + depth_ref[...].astype(jnp.float32)
    order_all = order_ref[...].astype(jnp.float32)
    cos_all = cos_ref[...].astype(jnp.float32)

    binned[bins * lat :, :] = jnp.zeros((binned.shape[0] - bins * lat, levels), jnp.float32)
    surface, incoming = [], []
    for i in range(lon):
        top = column_of(top_all[i : i + 1], lat)
        end = column_of(end_all[i : i + 1], lat)
        order = column_of(order_all[i : i + 1], lat)
        cosine = column_of(cos_all[i : i + 1], lat)
        lev = level_lane.astype(jnp.float32)
        cloudy = ((lev >= top) & (lev < end)).astype(jnp.float32)
        for b in range(bins):
            binned[b * lat : (b + 1) * lat, :] = spec_ref[i, b].astype(jnp.float32) * cloudy
        for j in range(lat):
            column = binned[pl.ds(j, tall, stride=lat), :]
            rows_ref[pl.ds(i * lat + j, levels, stride=lon * lat), :tall] = column.T
        surf = jnp.dot(
            albedo_ref[i].astype(jnp.bfloat16), onehot.astype(jnp.bfloat16),
            preferred_element_type=jnp.float32,
        )
        lit = (order >= 0.0).astype(jnp.float32)
        surface.append(jnp.pad(surf, ((0, 0), (0, wide - gpoints))))
        incoming.append(jnp.pad((cosine * lit) * solar_g, ((0, 0), (0, wide - gpoints))))

    def fill(chunk, slot):
        start = pl.multiple_of(chunk * block, block)
        lhs = rows_ref[pl.ds(start, block), :tall].astype(jnp.bfloat16)
        optics[slot] = jnp.dot(lhs, table[...], preferred_element_type=jnp.float32)

    count = levels // CHUNK
    fill(count - 1, (count - 1) % 2)

    def one_chunk(k, carry):
        chunk = count - 1 - k
        slot = lax.rem(chunk, 2)
        fill(jnp.maximum(chunk - 1, 0), 1 - slot)
        state = list(carry)
        for step in reversed(range(CHUNK)):
            gas = gas_levels[pl.ds(chunk * CHUNK + step, 1), :]
            for i in range(lon):
                r = (step * lon + i) * lat
                ext = optics[slot, r : r + lat, :wide].astype(jnp.bfloat16).astype(jnp.float32)
                sca = optics[slot, r : r + lat, wide:].astype(jnp.bfloat16).astype(jnp.float32)
                net, both = state[i]
                total = ext + gas
                a = total - sca
                b = total - 0.85 * sca
                p = a * b
                grow = p * (2.0 + p * (2.0 / 3.0 + p * (4.0 / 45.0)))
                slope = 2.0 + p * (4.0 / 3.0 + p * (4.0 / 15.0 + p * (8.0 / 315.0)))
                d_net = grow * net + (a * slope) * both
                d_both = grow * both + (b * slope) * net
                at = pl.multiple_of((chunk * CHUNK + step) * (lon * lat), lon * lat)
                steps[pl.ds(at + i * lat, lat), :] = d_net
                state[i] = (net + d_net, both + d_both)
        return tuple(state)

    start = tuple((1.0 - s, 1.0 + s) for s in surface)
    final = lax.fori_loop(0, count, one_chunk, start)
    weights = [2.0 * q / (net + both) for q, (net, both) in zip(incoming, final)]

    def sum_chunk(chunk, sums):
        sums = list(sums)
        for step in range(CHUNK):
            level = chunk * CHUNK + step
            at = pl.multiple_of(level * (lon * lat), lon * lat)
            here = level_lane == level
            for i in range(lon):
                part = steps[pl.ds(at + i * lat, lat), :] * weights[i]
                sums[i] = jnp.where(here, jnp.sum(part, axis=1, keepdims=True), sums[i])
        return tuple(sums)

    sums = lax.fori_loop(0, count, sum_chunk, tuple(jnp.zeros((lat, levels), jnp.float32) for _ in range(lon)))
    for i in range(lon):
        heat = sums[i] * factor_ref[...]
        heat_ref[i] = heat
        base_ref[i] = temp_ref[i] + heat


def shards(
    spectra, cloud_top, cloud_depth, sun_order, sunlit_cos, albedo, temp,
    extinction, scatter_albedo, gas_depth, band_map, solar_band, heat_factor,
):
    def shift(x, axis, by):
        n = lax.axis_size(axis)
        return lax.ppermute(x, axis, [(i, (i + by) % n) for i in range(n)])

    west = shift(temp, "col", 1)
    east = shift(temp, "col", -1)
    south = shift(temp, "gpt", 1)
    north = shift(temp, "gpt", -1)
    lon, lat, bins, levels = spectra.shape
    gpoints = extinction.shape[1]
    tall = -(-bins // 8) * 8
    shape = jax.ShapeDtypeStruct((lon, lat, levels), jnp.float32)
    heating, base = pl.pallas_call(
        radiation_kernel,
        out_shape=[shape, shape],
        scratch_shapes=[
            pltpu.VMEM((tall * lat, levels), jnp.float32),
            pltpu.VMEM((levels * lon * lat, 128), jnp.float32),
            pltpu.VMEM((2, CHUNK * lon * lat, 256), jnp.float32),
            pltpu.VMEM((levels, 128), jnp.float32),
            pltpu.VMEM((tall, 256), jnp.bfloat16),
            pltpu.VMEM((levels * lon * lat, 128), jnp.float32),
        ],
        compiler_params=pltpu.CompilerParams(vmem_limit_bytes=32 * 1024 * 1024),
        name="radiation",
    )(
        jnp.transpose(spectra, (0, 2, 1, 3)), cloud_top, cloud_depth, sun_order, sunlit_cos, albedo, temp,
        extinction, scatter_albedo, gas_depth, band_map[None], solar_band[None], heat_factor[None],
    )
    up = jnp.concatenate([west[lon - 1 :], temp[: lon - 1]], axis=0)
    down = jnp.concatenate([temp[1:], east[:1]], axis=0)
    left = jnp.concatenate([south[:, lat - 1 :], temp[:, : lat - 1]], axis=1)
    right = jnp.concatenate([temp[:, 1:], north[:, :1]], axis=1)
    return (heating, base + DIFFUSION * (up + down + left + right - 4.0 * temp))


def solution(mesh):
    column = P("col", "gpt")
    deep = P("col", "gpt", None)
    in_specs = (P("col", "gpt", None, None), column, column, column, column, deep, deep) + (P(),) * 6
    return jax.shard_map(shards, mesh=mesh, in_specs=in_specs, out_specs=(deep, deep), check_vma=False)
```

time: 170 us -> 21.8 us (0.13)
  the two profiles are of different devices: /device:TPU:1 before, /device:TPU:0 now
where the time goes in v1:
time: 21.8 us; the launch traced here: 21.6 us
  Pallas kernels  9.1 us (42%)
  starting transfers between devices  8.58 us (39%)
  local copies, waits for them, and re-layouts  2.48 us (11%)
  between operations  0.8 us (4%)
  other arithmetic  0.63 us (3%)
    pallas_call x1, Pallas kernels, shards(): pl.pallas_call(radiation_kernel, out_shape=[shape, shape], scratch_shapes...  9.1 us
    ppermute x4, starting transfers between devices, shift(): return lax.ppermute(x, axis, [(i, (i + by) % n) for i in range(n)])  8.58 us
    unnamed x26, local copies, waits for them, and re-layouts  1.67 us
    slice x2, local copies, waits for them, and re-layouts, shards(): right = jnp.concatenate([temp[:, 1:], north[:, :1]], axis=1)  0.79 us
    add x1, other arithmetic, shards(): return (heating, base + DIFFUSION * (up + down + left + right - 4.0 * temp))  0.63 us
  transfers between devices with their start and end apart: 4, of which 0 were waited for; matrix products, arithmetic and copies ran while one was open for 4% of the time, Pallas kernels for 42%

profile of v1, /device:TPU:0, one launch (start us, length us, event | category | flops | bytes accessed | tf_op | source)
XLA Modules:
  0.0 21.6 jit_solution(12258483223225003326)
XLA Ops:
  0.6 0.0 copy-start
  0.6 0.0 copy-start.2
  0.6 0.0 collective-permute-start.2
  0.7 5.4 %collective-permute-start.1 = (f32[4,8,128]{2,1,0:T(8,128)}, f32[4,8,128]{2,1,0:T(8,128)S(1)}, u32[]{:S(2)}, u32[]{:S(2)}) collective-permute-start(f32[4,8,128]{2,1,0:T(8,128)} %temp_ref.1), channel_id=1, source_target_pairs={{0,120},{8,0},{16,8},{24,16},{32,24},{40,32},{48,40},{56,48},{64,5... | collective-permute-start | bytes 49160 | tf_op jit(solution)/shard_map/ppermute | solution.py:136
  6.0 0.0 collective-permute-start
  6.0 3.2 %collective-permute-start.3 = (f32[4,8,128]{2,1,0:T(8,128)}, f32[4,8,128]{2,1,0:T(8,128)S(1)}, u32[]{:S(2)}, u32[]{:S(2)}) collective-permute-start(f32[4,8,128]{2,1,0:T(8,128)} %temp_ref.1), channel_id=1, source_target_pairs={{0,7},{1,0},{2,1},{3,2},{4,3},{5,4},{6,5},{7,6},{8,15},{9,8},{10,9... | collective-permute-start | bytes 49160 | tf_op jit(solution)/shard_map/ppermute | solution.py:136
  9.2 0.8 %fusion.5 = (f32[4,7,128]{2,1,0:T(8,128)S(1)}, f32[4,7,128]{2,1,0:T(8,128)S(1)}) fusion(f32[4,8,128]{2,1,0:T(8,128)} %temp_ref.1), kind=kLoop, calls=%fused_computation.6 | loop fusion | bytes 57344 | tf_op jit(solution)/shard_map/slice | solution.py:166
  10.0 0.0 copy-done
  10.0 0.0 copy-start.3
  10.0 0.0 copy-start.4
  10.0 0.0 copy-start.5
  10.1 0.0 copy-start.11
  10.1 0.0 copy-start.12
  10.1 0.0 copy-start.8
  10.1 0.0 copy-start.7
  10.1 0.0 copy-start.6
  10.1 0.0 copy-start.9
  10.1 0.0 copy-start.10
  10.2 0.0 copy-done.2
  10.2 0.6 %copy-done.3 = f32[33,112]{1,0:T(8,128)S(1)} copy-done((f32[33,112]{1,0:T(8,128)S(1)}, f32[33,112]{1,0:T(8,128)}, u32[]{:S(2)}) %copy-start.3) | copy-done | bytes 14808
  10.8 0.0 copy-done.4
  10.8 0.0 copy-done.5
  10.8 0.0 copy-done.11
  10.8 0.0 copy-done.12
  10.8 0.0 copy-done.8
  10.8 0.0 copy-done.7
  10.8 0.0 copy-done.6
  10.8 0.0 copy-done.9
  10.8 0.0 copy-done.10
  10.8 0.0 copy-start.1
  10.8 1.0 %copy-done.1 = bf16[4,8,33,128]{3,1,2,0:T(8,128)(2,1)S(1)} copy-done((bf16[4,8,33,128]{3,1,2,0:T(8,128)(2,1)S(1)}, bf16[4,8,33,128]{3,1,2,0:T(8,128)(2,1)}, u32[]{:S(2)}) %copy-start.1) | copy-done | bytes 270360
  11.8 9.1 %radiation.1 = (f32[4,8,128]{2,1,0:T(8,128)}, f32[4,8,128]{2,1,0:T(8,128)S(1)}) custom-call(bf16[4,33,8,128]{3,2,1,0:T(8,128)(2,1)S(1)} %bitcast.4, s32[4,8]{1,0:T(4,128)S(1)} %copy-done.6, s32[4,8]{1,0:T(4,128)S(1)} %copy-done.7, s32[4,8]{1,0:T(4,128)S(1)} %copy-done.8, bf16[4,8]{1,0:T(4,128)(2,1)S(1)} %copy-done.9, bf16[4,8,14]{2,1,0:T(8,128)(2,1)S(1)} %copy-done.5, ...), custom_call_target="tpu_custom_call" | custom-call | tf_op jit(solution)/shard_map/radiation/pallas_call | solution.py:146
  20.9 0.0 collective-permute-done.2
  20.9 0.0 collective-permute-done.1
  20.9 0.0 collective-permute-done
  20.9 0.0 collective-permute-done.3
  21.0 0.6 %fusion.4 = f32[4,8,128]{2,1,0:T(8,128)} fusion(f32[4,8,128]{2,1,0:T(8,128)S(1)} %get-tuple-element.5, f32[3,8,128]{2,1,0:T(8,128)S(1)} %get-tuple-element.9, f32[1,8,128]{2,1,0:T(8,128)S(1)} %slice.32, f32[1,8,128]{2,1,0:T(8,128)S(1)} %slice.33, f32[3,8,128]{2,1,0:T(8,128)S(1)} %get-tuple-element.8, f32[4,7,128]{2,1,0:T(8,128)S(1)} %get-tuple-element.7, ...), kind=kLoop, calls=%fused_computation.5 | loop fusion | flops 45056 | bytes 114688 | tf_op jit(solution)/shard_map/add | solution.py:167
  (5 shorter events, 0.0 us)
Async XLA Ops:
  0.6 9.4 %copy-start = (f32[4,8,128]{2,1,0:T(8,128)S(1)}, f32[4,8,128]{2,1,0:T(8,128)}, u32[]{:S(2)}) copy-start(f32[4,8,128]{2,1,0:T(8,128)} %temp_ref.1) | copy-start | bytes 49156
  0.6 9.5 %copy-start.2 = (f32[112,128]{1,0:T(8,128)S(1)}, f32[112,128]{1,0:T(8,128)}, u32[]{:S(2)}) copy-start(f32[112,128]{1,0:T(8,128)} %gas_ref.1) | copy-start | bytes 172036
  0.6 20.2 %collective-permute-start.2 = (f32[4,8,128]{2,1,0:T(8,128)}, f32[4,8,128]{2,1,0:T(8,128)S(1)}, u32[]{:S(2)}, u32[]{:S(2)}) collective-permute-start(f32[4,8,128]{2,1,0:T(8,128)} %temp_ref.1), channel_id=1, source_target_pairs={{0,1},{1,2},{2,3},{3,4},{4,5},{5,6},{6,7},{7,0},{8,9},{9,10},{10,1... | collective-permute-start | bytes 49160 | tf_op jit(solution)/shard_map/ppermute | solution.py:136
  0.7 20.2 %collective-permute-start.1 = (f32[4,8,128]{2,1,0:T(8,128)}, f32[4,8,128]{2,1,0:T(8,128)S(1)}, u32[]{:S(2)}, u32[]{:S(2)}) collective-permute-start(f32[4,8,128]{2,1,0:T(8,128)} %temp_ref.1), channel_id=1, source_target_pairs={{0,120},{8,0},{16,8},{24,16},{32,24},{40,32},{48,40},{56,48},{64,5... | collective-permute-start | bytes 49160 | tf_op jit(solution)/shard_map/ppermute | solution.py:136
  6.0 14.9 %collective-permute-start = (f32[4,8,128]{2,1,0:T(8,128)}, f32[4,8,128]{2,1,0:T(8,128)S(1)}, u32[]{:S(2)}, u32[]{:S(2)}) collective-permute-start(f32[4,8,128]{2,1,0:T(8,128)} %temp_ref.1), channel_id=1, source_target_pairs={{0,8},{8,16},{16,24},{24,32},{32,40},{40,48},{48,56},{56,64},{64,7... | collective-permute-start | bytes 49160 | tf_op jit(solution)/shard_map/ppermute | solution.py:136
  6.0 14.9 %collective-permute-start.3 = (f32[4,8,128]{2,1,0:T(8,128)}, f32[4,8,128]{2,1,0:T(8,128)S(1)}, u32[]{:S(2)}, u32[]{:S(2)}) collective-permute-start(f32[4,8,128]{2,1,0:T(8,128)} %temp_ref.1), channel_id=1, source_target_pairs={{0,7},{1,0},{2,1},{3,2},{4,3},{5,4},{6,5},{7,6},{8,15},{9,8},{10,9... | collective-permute-start | bytes 49160 | tf_op jit(solution)/shard_map/ppermute | solution.py:136
  10.0 0.7 %copy-start.3 = (f32[33,112]{1,0:T(8,128)S(1)}, f32[33,112]{1,0:T(8,128)}, u32[]{:S(2)}) copy-start(f32[33,112]{1,0:T(8,128)} %scat_ref.1) | copy-start | bytes 44356
  10.0 0.7 %copy-start.4 = (bf16[33,112]{1,0:T(8,128)(2,1)S(1)}, bf16[33,112]{1,0:T(8,128)(2,1)}, u32[]{:S(2)}) copy-start(bf16[33,112]{1,0:T(8,128)(2,1)} %ext_ref.1) | copy-start | bytes 22180
  10.0 0.7 %copy-start.5 = (bf16[4,8,14]{2,1,0:T(8,128)(2,1)S(1)}, bf16[4,8,14]{2,1,0:T(8,128)(2,1)}, u32[]{:S(2)}) copy-start(bf16[4,8,14]{2,1,0:T(8,128)(2,1)} %albedo_ref.1) | copy-start | bytes 2692
  10.1 0.7 %copy-start.11 = (f32[14]{0:T(128)S(1)}, f32[14]{0:T(128)}, u32[]{:S(2)}) copy-start(f32[14]{0:T(128)} %param.24) | copy-start | bytes 172
  10.1 0.7 %copy-start.12 = (f32[128]{0:T(128)S(1)}, f32[128]{0:T(128)}, u32[]{:S(2)}) copy-start(f32[128]{0:T(128)} %param.25) | copy-start | bytes 1540
  10.1 0.7 %copy-start.8 = (s32[4,8]{1,0:T(4,128)S(1)}, s32[4,8]{1,0:T(4,128)}, u32[]{:S(2)}) copy-start(s32[4,8]{1,0:T(4,128)} %order_ref.1) | copy-start | bytes 388
  10.1 0.7 %copy-start.7 = (s32[4,8]{1,0:T(4,128)S(1)}, s32[4,8]{1,0:T(4,128)}, u32[]{:S(2)}) copy-start(s32[4,8]{1,0:T(4,128)} %depth_ref.1) | copy-start | bytes 388
  10.1 0.7 %copy-start.6 = (s32[4,8]{1,0:T(4,128)S(1)}, s32[4,8]{1,0:T(4,128)}, u32[]{:S(2)}) copy-start(s32[4,8]{1,0:T(4,128)} %top_ref.1) | copy-start | bytes 388
  10.1 0.7 %copy-start.9 = (bf16[4,8]{1,0:T(4,128)(2,1)S(1)}, bf16[4,8]{1,0:T(4,128)(2,1)}, u32[]{:S(2)}) copy-start(bf16[4,8]{1,0:T(4,128)(2,1)} %cos_ref.1) | copy-start | bytes 196
  10.1 0.7 %copy-start.10 = (s32[112]{0:T(128)S(1)}, s32[112]{0:T(128)}, u32[]{:S(2)}) copy-start(s32[112]{0:T(128)} %param.23) | copy-start | bytes 1348
  10.8 1.0 %copy-start.1 = (bf16[4,8,33,128]{3,1,2,0:T(8,128)(2,1)S(1)}, bf16[4,8,33,128]{3,1,2,0:T(8,128)(2,1)}, u32[]{:S(2)}) copy-start(bf16[4,8,33,128]{3,1,2,0:T(8,128)(2,1)} %param.13) | copy-start | bytes 811012

commit v2 on v1

--- a/solution.py
+++ b/solution.py
@@ -8,6 +8,7 @@
 
 DIFFUSION = 0.2
 CHUNK = 8
+SUM_CHUNK = 32
 
 
 def column_of(row, size):
@@ -17,10 +18,10 @@
     return jnp.sum(jnp.where(lane == sublane, spread, jnp.zeros_like(spread)), axis=1, keepdims=True)
 
 
-def radiation_kernel(
-    spec_ref, top_ref, depth_ref, order_ref, cos_ref, albedo_ref, temp_ref,
+def radiate(
+    spec_ref, top_ref, depth_ref, order_ref, cos_ref, albedo_ref,
     ext_ref, scat_ref, gas_ref, band_ref, solar_ref, factor_ref,
-    heat_ref, base_ref,
+    heat_ref,
     binned, rows_ref, optics, gas_levels, table, steps,
 ):
     lon, bins, lat, levels = spec_ref.shape
@@ -72,25 +73,27 @@
         surface.append(jnp.pad(surf, ((0, 0), (0, wide - gpoints))))
         incoming.append(jnp.pad((cosine * lit) * solar_g, ((0, 0), (0, wide - gpoints))))
 
-    def fill(chunk, slot):
-        start = pl.multiple_of(chunk * block, block)
-        lhs = rows_ref[pl.ds(start, block), :tall].astype(jnp.bfloat16)
-        optics[slot] = jnp.dot(lhs, table[...], preferred_element_type=jnp.float32)
+    piece = 4 * block
+    for start_row in range(0, levels * lon * lat, piece):
+        lhs = rows_ref[start_row : start_row + piece, :tall].astype(jnp.bfloat16)
+        optics[start_row : start_row + piece, :] = jnp.dot(
+            lhs, table[...], preferred_element_type=jnp.float32
+        ).astype(jnp.bfloat16)
 
     count = levels // CHUNK
-    fill(count - 1, (count - 1) % 2)
 
     def one_chunk(k, carry):
         chunk = count - 1 - k
-        slot = lax.rem(chunk, 2)
-        fill(jnp.maximum(chunk - 1, 0), 1 - slot)
         state = list(carry)
         for step in reversed(range(CHUNK)):
             gas = gas_levels[pl.ds(chunk * CHUNK + step, 1), :]
+            at = pl.multiple_of((chunk * CHUNK + step) * (lon * lat), lon * lat)
+            ext_two = [optics[pl.ds(at + 2 * i * lat, 2 * lat), :wide].astype(jnp.float32) for i in range(lon // 2)]
+            sca_two = [optics[pl.ds(at + 2 * i * lat, 2 * lat), wide:].astype(jnp.float32) for i in range(lon // 2)]
             for i in range(lon):
-                r = (step * lon + i) * lat
-                ext = optics[slot, r : r + lat, :wide].astype(jnp.bfloat16).astype(jnp.float32)
-                sca = optics[slot, r : r + lat, wide:].astype(jnp.bfloat16).astype(jnp.float32)
+                half = slice((i % 2) * lat, (i % 2 + 1) * lat)
+                ext = ext_two[i // 2][half]
+                sca = sca_two[i // 2][half]
                 net, both = state[i]
                 total = ext + gas
                 a = total - sca
@@ -100,7 +103,6 @@
                 slope = 2.0 + p * (4.0 / 3.0 + p * (4.0 / 15.0 + p * (8.0 / 315.0)))
                 d_net = grow * net + (a * slope) * both
                 d_both = grow * both + (b * slope) * net
-                at = pl.multiple_of((chunk * CHUNK + step) * (lon * lat), lon * lat)
                 steps[pl.ds(at + i * lat, lat), :] = d_net
                 state[i] = (net + d_net, both + d_both)
         return tuple(state)
@@ -111,8 +113,8 @@
 
     def sum_chunk(chunk, sums):
         sums = list(sums)
-        for step in range(CHUNK):
-            level = chunk * CHUNK + step
+        for step in range(SUM_CHUNK):
+            level = chunk * SUM_CHUNK + step
             at = pl.multiple_of(level * (lon * lat), lon * lat)
             here = level_lane == level
             for i in range(lon):
@@ -120,51 +122,83 @@
                 sums[i] = jnp.where(here, jnp.sum(part, axis=1, keepdims=True), sums[i])
         return tuple(sums)
 
-    sums = lax.fori_loop(0, count, sum_chunk, tuple(jnp.zeros((lat, levels), jnp.float32) for _ in range(lon)))
+    sums = lax.fori_loop(0, levels // SUM_CHUNK, sum_chunk, tuple(jnp.zeros((lat, levels), jnp.float32) for _ in range(lon)))
     for i in range(lon):
-        heat = sums[i] * factor_ref[...]
-        heat_ref[i] = heat
-        base_ref[i] = temp_ref[i] + heat
+        heat_ref[i] = sums[i] * factor_ref[...]
+
+
+def radiation_kernel(*refs):
+    count = 13
+    sources, heat_ref, base_ref = refs[:count], refs[count], refs[count + 1]
+    held, scratch, arrived = refs[count + 2 : 2 * count + 2], refs[2 * count + 2 : -1], refs[-1]
+    copies = [pltpu.make_async_copy(s, h, arrived.at[n]) for n, (s, h) in enumerate(zip(sources, held))]
+    for copy in copies:
+        copy.start()
+    for copy in copies:
+        copy.wait()
+    radiate(*held[:-1], heat_ref, *scratch)
+    temp_ref = held[-1]
+    lon, lat, levels = temp_ref.shape
+    edge = jnp.zeros((1, levels), jnp.float32)
+    for i in range(lon):
+        here = temp_ref[i]
+        around = jnp.concatenate([edge, here[: lat - 1]], axis=0) + jnp.concatenate([here[1:], edge], axis=0)
+        if i > 0:
+            around += temp_ref[i - 1]
+        if i < lon - 1:
+            around += temp_ref[i + 1]
+        base_ref[i] = here + DIFFUSION * (around - 4.0 * here) + heat_ref[i]
 
 
 def shards(
     spectra, cloud_top, cloud_depth, sun_order, sunlit_cos, albedo, temp,
     extinction, scatter_albedo, gas_depth, band_map, solar_band, heat_factor,
 ):
-    def shift(x, axis, by):
+    def swap(axis, odd):
         n = lax.axis_size(axis)
-        return lax.ppermute(x, axis, [(i, (i + by) % n) for i in range(n)])
-
-    west = shift(temp, "col", 1)
-    east = shift(temp, "col", -1)
-    south = shift(temp, "gpt", 1)
-    north = shift(temp, "gpt", -1)
+        partner = [(i ^ 1) if odd == 0 else ((i + 1) % n if i % 2 else (i - 1) % n) for i in range(n)]
+        return lax.ppermute(temp, axis, list(enumerate(partner)))
+
+    col_a, col_b, gpt_a, gpt_b = swap("col", 0), swap("col", 1), swap("gpt", 0), swap("gpt", 1)
     lon, lat, bins, levels = spectra.shape
-    gpoints = extinction.shape[1]
     tall = -(-bins // 8) * 8
     shape = jax.ShapeDtypeStruct((lon, lat, levels), jnp.float32)
+    inputs = (
+        jnp.transpose(spectra, (0, 2, 1, 3)), cloud_top, cloud_depth, sun_order, sunlit_cos, albedo,
+        extinction, scatter_albedo, gas_depth, band_map[None], solar_band[None], heat_factor[None], temp,
+    )
     heating, base = pl.pallas_call(
         radiation_kernel,
         out_shape=[shape, shape],
-        scratch_shapes=[
+        in_specs=[pl.BlockSpec(memory_space=pltpu.HBM)] * len(inputs),
+        scratch_shapes=[pltpu.VMEM(x.shape, x.dtype) for x in inputs]
+        + [
             pltpu.VMEM((tall * lat, levels), jnp.float32),
             pltpu.VMEM((levels * lon * lat, 128), jnp.float32),
-            pltpu.VMEM((2, CHUNK * lon * lat, 256), jnp.float32),
+            pltpu.VMEM((levels * lon * lat, 256), jnp.bfloat16),
             pltpu.VMEM((levels, 128), jnp.float32),
             pltpu.VMEM((tall, 256), jnp.bfloat16),
             pltpu.VMEM((levels * lon * lat, 128), jnp.float32),
+            pltpu.SemaphoreType.DMA((len(inputs),)),
         ],
-        compiler_params=pltpu.CompilerParams(vmem_limit_bytes=32 * 1024 * 1024),
+        compiler_params=pltpu.CompilerParams(vmem_limit_bytes=60 * 1024 * 1024),
+        cost_estimate=pl.CostEstimate(flops=200_000_000, bytes_accessed=1 << 20, transcendentals=0),
         name="radiation",
-    )(
-        jnp.transpose(spectra, (0, 2, 1, 3)), cloud_top, cloud_depth, sun_order, sunlit_cos, albedo, temp,
-        extinction, scatter_albedo, gas_depth, band_map[None], solar_band[None], heat_factor[None],
+    )(*inputs)
+    col_a, col_b, gpt_a, gpt_b, base = lax.optimization_barrier((col_a, col_b, gpt_a, gpt_b, base))
+    col_even = lax.rem(lax.axis_index("col"), 2) == 0
+    gpt_even = lax.rem(lax.axis_index("gpt"), 2) == 0
+    west = jnp.where(col_even, col_b[lon - 1 :], col_a[lon - 1 :])
+    east = jnp.where(col_even, col_a[:1], col_b[:1])
+    south = jnp.where(gpt_even, gpt_b[:, lat - 1 :], gpt_a[:, lat - 1 :])
+    north = jnp.where(gpt_even, gpt_a[:, :1], gpt_b[:, :1])
+    temp_next = base + DIFFUSION * (
+        jnp.pad(west, ((0, lon - 1), (0, 0), (0, 0)))
+        + jnp.pad(east, ((lon - 1, 0), (0, 0), (0, 0)))
+        + jnp.pad(south, ((0, 0), (0, lat - 1), (0, 0)))
+        + jnp.pad(north, ((0, 0), (lat - 1, 0), (0, 0)))
     )
-    up = jnp.concatenate([west[lon - 1 :], temp[: lon - 1]], axis=0)
-    down = jnp.concatenate([temp[1:], east[:1]], axis=0)
-    left = jnp.concatenate([south[:, lat - 1 :], temp[:, : lat - 1]], axis=1)
-    right = jnp.concatenate([temp[:, 1:], north[:, :1]], axis=1)
-    return (heating, base + DIFFUSION * (up + down + left + right - 4.0 * temp))
+    return (heating, temp_next)
 
 
 def solution(mesh):

time: 21.8 us -> 19.2 us (0.88)
  the two profiles are of different devices: /device:TPU:0 before, /device:TPU:1 now
where the time goes in v2:
time: 19.2 us; the launch traced here: 19 us
  starting transfers between devices  9.99 us (52%)
  Pallas kernels  6.95 us (36%)
  local copies, waits for them, and re-layouts  0.7 us (4%)
  between operations  0.7 us (4%)
  other arithmetic  0.63 us (3%)
    ppermute x4, starting transfers between devices, swap(): return lax.ppermute(temp, axis, list(enumerate(partner)))  9.99 us
    pallas_call x1, Pallas kernels, shards(): pl.pallas_call(radiation_kernel, out_shape=[shape, shape], in_specs=[pl.B...  6.95 us
    unnamed x2, local copies, waits for them, and re-layouts  0.7 us
    add x1, other arithmetic, shards(): base + DIFFUSION * (jnp.pad(west, ((0, lon - 1), (0, 0), (0, 0))) + jnp.p...  0.61 us
  transfers between devices with their start and end apart: 4, of which 0 were waited for; matrix products, arithmetic and copies ran while one was open for 0% of the time, Pallas kernels for 37%

profile of v2, /device:TPU:1, one launch (start us, length us, event | category | flops | bytes accessed | tf_op | source)
XLA Modules:
  0.0 19.0 jit_solution(9969835583940845776)
XLA Ops:
  0.6 5.8 %collective-permute-start.1 = (f32[4,8,128]{2,1,0:T(8,128)}, f32[4,8,128]{2,1,0:T(8,128)S(1)}, u32[]{:S(2)}, u32[]{:S(2)}) collective-permute-start(f32[4,8,128]{2,1,0:T(8,128)} %refs_12_.1), channel_id=1, source_target_pairs={{0,120},{8,16},{16,8},{24,32},{32,24},{40,48},{48,40},{56,64},{64,... | collective-permute-start | bytes 49160 | tf_op jit(solution)/shard_map/ppermute | solution.py:160
  6.5 0.0 collective-permute-start
  6.5 2.5 %collective-permute-start.3 = (f32[4,8,128]{2,1,0:T(8,128)}, f32[4,8,128]{2,1,0:T(8,128)S(1)}, u32[]{:S(2)}, u32[]{:S(2)}) collective-permute-start(f32[4,8,128]{2,1,0:T(8,128)} %refs_12_.1), channel_id=1, source_target_pairs={{0,7},{1,2},{2,1},{3,4},{4,3},{5,6},{6,5},{7,0},{8,15},{9,10},{10,... | collective-permute-start | bytes 49160 | tf_op jit(solution)/shard_map/ppermute | solution.py:160
  9.0 1.7 %collective-permute-start.2 = (f32[4,8,128]{2,1,0:T(8,128)}, f32[4,8,128]{2,1,0:T(8,128)S(1)}, u32[]{:S(2)}, u32[]{:S(2)}) collective-permute-start(f32[4,8,128]{2,1,0:T(8,128)} %refs_12_.1), channel_id=1, source_target_pairs={{0,1},{1,0},{2,3},{3,2},{4,5},{5,4},{6,7},{7,6},{8,9},{9,8},{10,11... | collective-permute-start | bytes 49160 | tf_op jit(solution)/shard_map/ppermute | solution.py:160
  10.6 7.0 %radiation.1 = (f32[4,8,128]{2,1,0:T(8,128)}, f32[4,8,128]{2,1,0:T(8,128)}) custom-call(bf16[4,33,8,128]{3,2,1,0:T(8,128)(2,1)} %bitcast.4, s32[4,8]{1,0:T(4,128)} %refs_1_.1, s32[4,8]{1,0:T(4,128)} %refs_2_.1, s32[4,8]{1,0:T(4,128)} %refs_3_.1, bf16[4,8]{1,0:T(4,128)(2,1)} %refs_4_.1, bf16[4,8,14]{2,1,0:T(8,128)(2,1)} %refs_5_.1, bf16[33,112]{1,0:T(8,128)(2,1)} %refs_6_.1, ...), custom_call_target="tpu_custom_call" | custom-call | flops 200000000 | bytes 1048576 | tf_op jit(solution)/shard_map/radiation/pallas_call | solution.py:170
  17.6 0.0 collective-permute-done.1
  17.6 0.0 collective-permute-done
  17.6 0.0 collective-permute-done.3
  17.6 0.0 collective-permute-done.2
  17.7 0.0 copy-start
  17.7 0.7 %copy-done = f32[4,8,128]{2,1,0:T(8,128)S(1)} copy-done((f32[4,8,128]{2,1,0:T(8,128)S(1)}, f32[4,8,128]{2,1,0:T(8,128)}, u32[]{:S(2)}) %copy-start) | copy-done | bytes 16408
  18.4 0.6 %multiply_add_fusion = f32[4,8,128]{2,1,0:T(8,128)} fusion(f32[4,8,128]{2,1,0:T(8,128)S(1)} %copy-done, f32[4,1,128]{2,1,0:T(1,128)S(1)} %get-tuple-element.19, f32[4,1,128]{2,1,0:T(1,128)S(1)} %get-tuple-element.18, f32[1,8,128]{2,1,0:T(8,128)S(1)} %get-tuple-element.17, f32[1,8,128]{2,1,0:T(8,128)S(1)} %get-tuple-element.16), kind=kLoop, calls=%fused_computation | loop fusion | flops 20480 | bytes 45056 | tf_op jit(solution)/shard_map/add | solution.py:195
  (2 shorter events, 0.0 us)
Async XLA Ops:
  0.6 17.0 %collective-permute-start.1 = (f32[4,8,128]{2,1,0:T(8,128)}, f32[4,8,128]{2,1,0:T(8,128)S(1)}, u32[]{:S(2)}, u32[]{:S(2)}) collective-permute-start(f32[4,8,128]{2,1,0:T(8,128)} %refs_12_.1), channel_id=1, source_target_pairs={{0,120},{8,16},{16,8},{24,32},{32,24},{40,48},{48,40},{56,64},{64,... | collective-permute-start | bytes 49160 | tf_op jit(solution)/shard_map/ppermute | solution.py:160
  6.5 11.1 %collective-permute-start = (f32[4,8,128]{2,1,0:T(8,128)}, f32[4,8,128]{2,1,0:T(8,128)S(1)}, u32[]{:S(2)}, u32[]{:S(2)}) collective-permute-start(f32[4,8,128]{2,1,0:T(8,128)} %refs_12_.1), channel_id=1, source_target_pairs={{0,8},{8,0},{16,24},{24,16},{32,40},{40,32},{48,56},{56,48},{64,72... | collective-permute-start | bytes 49160 | tf_op jit(solution)/shard_map/ppermute | solution.py:160
  6.5 11.1 %collective-permute-start.3 = (f32[4,8,128]{2,1,0:T(8,128)}, f32[4,8,128]{2,1,0:T(8,128)S(1)}, u32[]{:S(2)}, u32[]{:S(2)}) collective-permute-start(f32[4,8,128]{2,1,0:T(8,128)} %refs_12_.1), channel_id=1, source_target_pairs={{0,7},{1,2},{2,1},{3,4},{4,3},{5,6},{6,5},{7,0},{8,15},{9,10},{10,... | collective-permute-start | bytes 49160 | tf_op jit(solution)/shard_map/ppermute | solution.py:160
  9.0 8.7 %collective-permute-start.2 = (f32[4,8,128]{2,1,0:T(8,128)}, f32[4,8,128]{2,1,0:T(8,128)S(1)}, u32[]{:S(2)}, u32[]{:S(2)}) collective-permute-start(f32[4,8,128]{2,1,0:T(8,128)} %refs_12_.1), channel_id=1, source_target_pairs={{0,1},{1,0},{2,3},{3,2},{4,5},{5,4},{6,7},{7,6},{8,9},{9,8},{10,11... | collective-permute-start | bytes 49160 | tf_op jit(solution)/shard_map/ppermute | solution.py:160
  17.7 0.7 %copy-start = (f32[4,8,128]{2,1,0:T(8,128)S(1)}, f32[4,8,128]{2,1,0:T(8,128)}, u32[]{:S(2)}) copy-start(f32[4,8,128]{2,1,0:T(8,128)} %get-tuple-element.11) | copy-start | bytes 49156

commit v3 on v2

v3 whole, which is shorter than its diff:
```python
import jax
import jax.numpy as jnp
from jax import lax
from jax.experimental import pallas as pl
from jax.experimental.pallas import tpu as pltpu
from jax.sharding import PartitionSpec as P

DIFFUSION = 0.2
CHUNK = 8
PAIR = 2
INPUTS = 13
WIDE = 128


def column_of(row, size):
    spread = jnp.broadcast_to(row, (size, size))
    lane = lax.broadcasted_iota(jnp.int32, (size, size), 1)
    sublane = lax.broadcasted_iota(jnp.int32, (size, size), 0)
    return jnp.sum(jnp.where(lane == sublane, spread, jnp.zeros_like(spread)), axis=1, keepdims=True)


def radiate(
    first, last,
    spec_ref, top_ref, depth_ref, order_ref, cos_ref, albedo_ref,
    ext_ref, scat_ref, gas_ref, band_ref, solar_ref, factor_ref, top_scalars,
    heat_ref,
    binned, rows_ref, optics, gas_levels, table, steps, flat, gas_window, e_levels, clear_high, clear_low, ends,
):
    lon, bins, lat, levels = spec_ref.shape
    gpoints = ext_ref.shape[1]
    bands = albedo_ref.shape[2]
    tall = binned.shape[0] // lat
    group = PAIR * lat
    window = levels // 2

    table[...] = jnp.zeros_like(table)
    ext = ext_ref[...]
    table[:bins, :gpoints] = ext
    table[:bins, WIDE : WIDE + gpoints] = (ext.astype(jnp.float32) * scat_ref[...]).astype(jnp.bfloat16)

    gas = jnp.pad(gas_ref[...], ((0, WIDE - gpoints), (0, 0)))
    under = lax.broadcasted_iota(jnp.int32, (levels, levels), 0) > lax.broadcasted_iota(jnp.int32, (levels, levels), 1)
    below = jnp.dot(
        gas, under.astype(jnp.float32), precision=lax.Precision.HIGHEST, preferred_element_type=jnp.float32
    )
    t = 2.0 * gas
    rise = t * (1.0 + t * (0.5 + t * (1.0 / 6.0 + t * (1.0 / 24.0))))
    growth_below = jnp.exp(2.0 * below)
    growth = growth_below * (1.0 + rise)
    gas_levels[...] = gas.T
    e_levels[...] = growth.T
    for n, part in enumerate((growth_below * rise, rise / growth)):
        high = part.astype(jnp.bfloat16)
        clear_high[n * WIDE : (n + 1) * WIDE, :] = high
        clear_low[n * WIDE : (n + 1) * WIDE, :] = (part - high.astype(jnp.float32)).astype(jnp.bfloat16)

    onehot = (
        lax.broadcasted_iota(jnp.int32, (bands, gpoints), 0) == band_ref[...]
    ).astype(jnp.float32)
    solar_g = jnp.dot(
        solar_ref[...], onehot, precision=lax.Precision.HIGHEST, preferred_element_type=jnp.float32
    )
    onehot = onehot.astype(jnp.bfloat16)
    lev = lax.broadcasted_iota(jnp.int32, (lat, levels), 1).astype(jnp.float32)
    top = top_ref[...].astype(jnp.float32)
    flat[0, :lon, :lat] = top
    flat[1, :lon, :lat] = top + depth_ref[...].astype(jnp.float32)
    flat[2, :lon, :lat] = order_ref[...].astype(jnp.float32)
    flat[3, :lon, :lat] = cos_ref[...].astype(jnp.float32)
    binned[bins * lat :, :] = jnp.zeros((binned.shape[0] - bins * lat, levels), jnp.float32)

    def one_pair(pair, nothing):
        surface, incoming, tops = [], [], []
        for i in range(PAIR):
            at_lon = pair * PAIR + i
            top, end, order, cosine = (column_of(flat[n, pl.ds(at_lon, 1), :lat], lat) for n in range(4))
            cloudy = ((lev >= top) & (lev < end)).astype(jnp.float32)
            for b in range(bins):
                binned[b * lat : (b + 1) * lat, :] = spec_ref[at_lon, b].astype(jnp.float32) * cloudy
            for j in range(lat):
                c = i * lat + j
                start = top_scalars[at_lon, j]
                column = pltpu.roll(binned[pl.ds(j, tall, stride=lat), :], lax.rem(levels - start, levels), 1)
                rows_ref[pl.ds(c, window, stride=group), :tall] = column.T[:window]
                gas_window[pl.ds(c, window, stride=group), :] = gas_levels[pl.ds(start, window), :]
                ends[0, c : c + 1, :] = e_levels[pl.ds(start, 1), :]
                ends[1, c : c + 1, :] = e_levels[pl.ds(start + window, 1), :]
            surf = jnp.dot(albedo_ref[at_lon], onehot, preferred_element_type=jnp.float32)
            lit = (order >= 0.0).astype(jnp.float32)
            surface.append(jnp.pad(surf, ((0, 0), (0, WIDE - gpoints))))
            incoming.append(jnp.pad((cosine * lit) * solar_g, ((0, 0), (0, WIDE - gpoints))))
            tops.append(top)

        lhs = rows_ref[:, :tall].astype(jnp.bfloat16)
        optics[...] = jnp.dot(lhs, table[...], preferred_element_type=jnp.float32).astype(jnp.bfloat16)

        def one_chunk(k, carry):
            chunk = window // CHUNK - 1 - k
            state = list(carry)
            for step in reversed(range(CHUNK)):
                at = pl.multiple_of((chunk * CHUNK + step) * group, group)
                ext_pair = optics[pl.ds(at, group), :WIDE].astype(jnp.float32)
                sca_pair = optics[pl.ds(at, group), WIDE:].astype(jnp.float32)
                for i in range(PAIR):
                    ext, sca = ext_pair[i * lat : (i + 1) * lat], sca_pair[i * lat : (i + 1) * lat]
                    net, both = state[i]
                    total = ext + gas_window[pl.ds(at + i * lat, lat), :]
                    a = total - sca
                    b = total - 0.85 * sca
                    p = a * b
                    grow = p * (2.0 + p * (2.0 / 3.0 + p * (4.0 / 45.0)))
                    slope = 2.0 + p * (4.0 / 3.0 + p * (4.0 / 15.0 + p * (8.0 / 315.0)))
                    d_net = grow * net + (a * slope) * both
                    d_both = grow * both + (b * slope) * net
                    steps[pl.ds(at + i * lat, lat), :] = d_net
                    state[i] = (net + d_net, both + d_both)
            return tuple(state)

        begin = []
        for i in range(PAIR):
            e_end = ends[1, i * lat : (i + 1) * lat, :]
            upward = surface[i] / e_end
            begin.append((e_end - upward, e_end + upward))
        final = lax.fori_loop(0, window // CHUNK, one_chunk, tuple(begin))

        weights, clear = [], []
        for i, (net, both) in enumerate(final):
            e_top = ends[0, i * lat : (i + 1) * lat, :]
            over = incoming[i] / e_levels[:1, :]
            weight = 2.0 * over * e_top / (net + both)
            weights.append(weight)
            clear.append(jnp.concatenate([over, 0.5 * weight * (both - net) * e_top], axis=1))
            clear.append(jnp.concatenate([weight, weight * surface[i]], axis=1))
        clear = jnp.concatenate(clear, axis=0)
        high = clear.astype(jnp.bfloat16)
        low = (clear - high.astype(jnp.float32)).astype(jnp.bfloat16)
        outside = (
            jnp.dot(high, clear_high[...], preferred_element_type=jnp.float32)
            + jnp.dot(high, clear_low[...], preferred_element_type=jnp.float32)
            + jnp.dot(low, clear_high[...], preferred_element_type=jnp.float32)
        )

        for i in range(PAIR):
            place = lev - tops[i]
            sums = jnp.where(place < 0.0, outside[2 * i * lat : (2 * i + 1) * lat],
                             outside[(2 * i + 1) * lat : (2 * i + 2) * lat])
            for k in range(window):
                part = steps[k * group + i * lat : k * group + (i + 1) * lat, :] * weights[i]
                sums = jnp.where(place == float(k), jnp.sum(part, axis=1, keepdims=True), sums)
            heat_ref[pair * PAIR + i] = sums * factor_ref[...]
        return nothing

    lax.fori_loop(first, last, one_pair, 0)


def pairs_ahead():
    at_col, at_gpt = lax.axis_index("col"), lax.axis_index("gpt")
    y, x, z = at_col // 4, lax.rem(at_col, 4), at_gpt // 2
    place = 8 * x + 9 * y + 13 * z
    return jnp.where(place <= -1, 2, jnp.where(place <= 30, 1, 0))


def fetch(sources, held, arrived):
    copies = [pltpu.make_async_copy(s, h, arrived.at[n]) for n, (s, h) in enumerate(zip(sources, held))]
    for copy in copies:
        copy.start()
    for copy in copies:
        copy.wait()


def ahead_kernel(*refs):
    count = INPUTS
    sources, out_ref = refs[:count], refs[count]
    held, heat_ref = refs[count + 1 : 2 * count + 1], refs[2 * count + 1]
    scratch, arrived = refs[2 * count + 2 : -1], refs[-1]
    pairs = pairs_ahead()

    @pl.when(pairs > 0)
    def _():
        fetch(sources, held, arrived)
        radiate(0, pairs, *held, heat_ref, *scratch)
        leave = pltpu.make_async_copy(heat_ref, out_ref, arrived.at[0])
        leave.start()
        leave.wait()


def after_kernel(temp_ref, early_ref, *refs):
    count = INPUTS
    sources, (heat_ref, base_ref) = refs[:count], refs[count : count + 2]
    held, scratch = refs[count + 2 : 2 * count + 2], refs[2 * count + 2 : -3]
    own_ref, two, arrived = refs[-3:]
    lon, lat, levels = temp_ref.shape
    pairs = pairs_ahead()
    early = pltpu.make_async_copy(early_ref, heat_ref, two.at[0])
    early.start()
    own = pltpu.make_async_copy(temp_ref, own_ref, two.at[1])
    own.start()

    @pl.when(pairs < lon // PAIR)
    def _():
        fetch(sources, held, arrived)

    early.wait()
    own.wait()
    temp_ref = own_ref

    @pl.when(pairs < lon // PAIR)
    def _():
        radiate(pairs, lon // PAIR, *held, heat_ref, *scratch)

    edge = jnp.zeros((1, levels), jnp.float32)
    for i in range(lon):
        here = temp_ref[i]
        around = jnp.concatenate([edge, here[: lat - 1]], axis=0) + jnp.concatenate([here[1:], edge], axis=0)
        if i > 0:
            around += temp_ref[i - 1]
        if i < lon - 1:
            around += temp_ref[i + 1]
        base_ref[i] = here + DIFFUSION * (around - 4.0 * here) + heat_ref[i]


def shards(
    spectra, cloud_top, cloud_depth, sun_order, sunlit_cos, albedo, temp,
    extinction, scatter_albedo, gas_depth, band_map, solar_band, heat_factor,
):
    lon, lat, bins, levels = spectra.shape
    tall = -(-bins // 8) * 8
    rows = levels // 2 * PAIR * lat
    shape = jax.ShapeDtypeStruct((lon, lat, levels), jnp.float32)
    inputs = (
        jnp.transpose(spectra, (0, 2, 1, 3)), cloud_top, cloud_depth, sun_order, sunlit_cos, albedo,
        extinction, scatter_albedo, gas_depth, band_map[None], solar_band[None], heat_factor[None],
        cloud_top,
    )
    apart = [pl.BlockSpec(memory_space=pltpu.HBM)] * len(inputs)
    held = [pltpu.VMEM(x.shape, x.dtype) for x in inputs[:-1]] + [pltpu.SMEM(cloud_top.shape, cloud_top.dtype)]
    scratch = [
        pltpu.VMEM((tall * lat, levels), jnp.float32),
        pltpu.VMEM((rows, WIDE), jnp.float32),
        pltpu.VMEM((rows, 2 * WIDE), jnp.bfloat16),
        pltpu.VMEM((levels, WIDE), jnp.float32),
        pltpu.VMEM((tall, 2 * WIDE), jnp.bfloat16),
        pltpu.VMEM((rows, WIDE), jnp.float32),
        pltpu.VMEM((4, 8, WIDE), jnp.float32),
        pltpu.VMEM((rows, WIDE), jnp.float32),
        pltpu.VMEM((levels, WIDE), jnp.float32),
        pltpu.VMEM((2 * WIDE, levels), jnp.bfloat16),
        pltpu.VMEM((2 * WIDE, levels), jnp.bfloat16),
        pltpu.VMEM((2, PAIR * lat, WIDE), jnp.float32),
        pltpu.SemaphoreType.DMA((len(inputs),)),
    ]
    params = pltpu.CompilerParams(vmem_limit_bytes=60 * 1024 * 1024)
    early = pl.pallas_call(
        ahead_kernel,
        out_shape=shape,
        in_specs=apart,
        out_specs=pl.BlockSpec(memory_space=pltpu.HBM),
        scratch_shapes=held + [pltpu.VMEM(shape.shape, shape.dtype)] + scratch,
        compiler_params=params,
        name="radiation_ahead",
    )(*inputs)
    sent, early = lax.optimization_barrier((temp, early))

    def swap(axis, odd):
        n = lax.axis_size(axis)
        partner = [(i ^ 1) if odd == 0 else ((i + 1) % n if i % 2 else (i - 1) % n) for i in range(n)]
        return lax.ppermute(sent, axis, list(enumerate(partner)))

    col_a, col_b, gpt_a, gpt_b = swap("col", 0), swap("col", 1), swap("gpt", 0), swap("gpt", 1)
    heating, base = pl.pallas_call(
        after_kernel,
        out_shape=[shape, shape],
        in_specs=apart[:2] + apart,
        scratch_shapes=held
        + scratch[:-1]
        + [pltpu.VMEM(shape.shape, shape.dtype), pltpu.SemaphoreType.DMA((2,)), scratch[-1]],
        compiler_params=params,
        cost_estimate=pl.CostEstimate(flops=200_000_000, bytes_accessed=1 << 20, transcendentals=0),
        name="radiation_after",
    )(temp, early, *inputs)
    gpt_a, col_b, col_a, gpt_b = lax.optimization_barrier((gpt_a, col_b, col_a, gpt_b))
    base = lax.optimization_barrier(base)
    col_even = lax.rem(lax.axis_index("col"), 2) == 0
    gpt_even = lax.rem(lax.axis_index("gpt"), 2) == 0
    west = jnp.where(col_even, col_b[lon - 1 :], col_a[lon - 1 :])
    east = jnp.where(col_even, col_a[:1], col_b[:1])
    south = jnp.where(gpt_even, gpt_b[:, lat - 1 :], gpt_a[:, lat - 1 :])
    north = jnp.where(gpt_even, gpt_a[:, :1], gpt_b[:, :1])
    temp_next = base + DIFFUSION * (
        jnp.pad(west, ((0, lon - 1), (0, 0), (0, 0)))
        + jnp.pad(east, ((lon - 1, 0), (0, 0), (0, 0)))
        + jnp.pad(south, ((0, 0), (0, lat - 1), (0, 0)))
        + jnp.pad(north, ((0, 0), (lat - 1, 0), (0, 0)))
    )
    return (heating, temp_next)


def solution(mesh):
    column = P("col", "gpt")
    deep = P("col", "gpt", None)
    in_specs = (P("col", "gpt", None, None), column, column, column, column, deep, deep) + (P(),) * 6
    return jax.shard_map(shards, mesh=mesh, in_specs=in_specs, out_specs=(deep, deep), check_vma=False)
```

time: 19.2 us -> 16.2 us (0.84)
  starting transfers between devices: 9.99 us -> 6.18 us
  Pallas kernels: 6.95 us -> 7.62 us
    ppermute x4, starting transfers between devices: 9.99 us -> 6.18 us  [swap(): return lax.ppermute(sent, axis, list(enumerate(partner)))]
    pallas_call x1 -> x2, Pallas kernels: 6.95 us -> 7.62 us  [the longest x1 3.81 us: shards(): pl.pallas_call(after_kernel, out_shape=[shape, shape], in_specs=apart[:2]...]
    unnamed x2 -> x4, local copies, waits for them, and re-layouts: 0.7 us -> 0.7 us
  transfers between devices with their start and end apart: 4 -> 4, of which waited for: 0 -> 0; matrix products, arithmetic and copies ran while one was open for 0% -> 0% of each run, Pallas kernels for 37% -> 24%
where the time goes in v3:
time: 16.2 us; the launch traced here: 15.9 us
  Pallas kernels  7.62 us (47%)
  starting transfers between devices  6.18 us (38%)
  between operations  0.72 us (4%)
  local copies, waits for them, and re-layouts  0.7 us (4%)
  other arithmetic  0.63 us (4%)
    ppermute x4, starting transfers between devices, swap(): return lax.ppermute(sent, axis, list(enumerate(partner)))  6.18 us
    pallas_call x1, Pallas kernels, shards(): pl.pallas_call(after_kernel, out_shape=[shape, shape], in_specs=apart[:2]...  3.81 us
    pallas_call x1, Pallas kernels, shards(): pl.pallas_call(ahead_kernel, out_shape=shape, in_specs=apart, out_specs=p...  3.81 us
    unnamed x4, local copies, waits for them, and re-layouts  0.7 us
    add x1, other arithmetic, shards(): base + DIFFUSION * (jnp.pad(west, ((0, lon - 1), (0, 0), (0, 0))) + jnp.p...  0.61 us
  transfers between devices with their start and end apart: 4, of which 0 were waited for; matrix products, arithmetic and copies ran while one was open for 0% of the time, Pallas kernels for 24%

profile of v3, /device:TPU:1, one launch (start us, length us, event | category | flops | bytes accessed | tf_op | source)
XLA Modules:
  0.0 15.9 jit_solution(11169552722310350650)
XLA Ops:
  0.6 0.0 copy-start.1
  0.6 3.8 %radiation_ahead.1.early_ref = f32[4,8,128]{2,1,0:T(8,128)} custom-call(bf16[4,33,8,128]{3,2,1,0:T(8,128)(2,1)} %bitcast.4, s32[4,8]{1,0:T(4,128)} %refs_12_.3, s32[4,8]{1,0:T(4,128)} %refs_2_.3, s32[4,8]{1,0:T(4,128)} %refs_3_.3, bf16[4,8]{1,0:T(4,128)(2,1)} %refs_4_.3, bf16[4,8,14]{2,1,0:T(8,128)(2,1)} %refs_5_.3, bf16[33,112]{1,0:T(8,128)(2,1)} %refs_6_.3, ...), custom_call_target="tpu_custom_call" | custom-call | tf_op jit(solution)/shard_map/radiation_ahead/pallas_call | solution.py:253
  4.5 0.0 copy-done.1
  4.5 1.5 %collective-permute-start = (f32[4,8,128]{2,1,0:T(8,128)S(1)}, f32[4,8,128]{2,1,0:T(8,128)S(1)}, u32[]{:S(2)}, u32[]{:S(2)}) collective-permute-start(f32[4,8,128]{2,1,0:T(8,128)S(1)} %copy-done.1), channel_id=1, source_target_pairs={{0,1},{1,0},{2,3},{3,2},{4,5},{5,4},{6,7},{7,6},{8,9},{9,8},{10,11... | collective-permute-start | bytes 49160 | tf_op jit(solution)/shard_map/ppermute | solution.py:267
  6.0 1.8 %collective-permute-start.1 = (f32[4,8,128]{2,1,0:T(8,128)S(1)}, f32[4,8,128]{2,1,0:T(8,128)S(1)}, u32[]{:S(2)}, u32[]{:S(2)}) collective-permute-start(f32[4,8,128]{2,1,0:T(8,128)S(1)} %copy-done.1), channel_id=1, source_target_pairs={{0,120},{8,16},{16,8},{24,32},{32,24},{40,48},{48,40},{56,64},{64,... | collective-permute-start | bytes 49160 | tf_op jit(solution)/shard_map/ppermute | solution.py:267
  7.8 0.7 %collective-permute-start.2 = (f32[4,8,128]{2,1,0:T(8,128)S(1)}, f32[4,8,128]{2,1,0:T(8,128)S(1)}, u32[]{:S(2)}, u32[]{:S(2)}) collective-permute-start(f32[4,8,128]{2,1,0:T(8,128)S(1)} %copy-done.1), channel_id=1, source_target_pairs={{0,8},{8,0},{16,24},{24,16},{32,40},{40,32},{48,56},{56,48},{64,72... | collective-permute-start | bytes 49160 | tf_op jit(solution)/shard_map/ppermute | solution.py:267
  8.5 2.2 %collective-permute-start.3 = (f32[4,8,128]{2,1,0:T(8,128)S(1)}, f32[4,8,128]{2,1,0:T(8,128)S(1)}, u32[]{:S(2)}, u32[]{:S(2)}) collective-permute-start(f32[4,8,128]{2,1,0:T(8,128)S(1)} %copy-done.1), channel_id=1, source_target_pairs={{0,7},{1,2},{2,1},{3,4},{4,3},{5,6},{6,5},{7,0},{8,15},{9,10},{10,... | collective-permute-start | bytes 49160 | tf_op jit(solution)/shard_map/ppermute | solution.py:267
  10.6 3.8 %radiation_after.1 = (f32[4,8,128]{2,1,0:T(8,128)}, f32[4,8,128]{2,1,0:T(8,128)}) custom-call(f32[4,8,128]{2,1,0:T(8,128)} %temp_ref.1, f32[4,8,128]{2,1,0:T(8,128)} %radiation_ahead.1.early_ref, bf16[4,33,8,128]{3,2,1,0:T(8,128)(2,1)} %bitcast.5, s32[4,8]{1,0:T(4,128)} %refs_12_.3, s32[4,8]{1,0:T(4,128)} %refs_2_.3, s32[4,8]{1,0:T(4,128)} %refs_3_.3, ...), custom_call_target="tpu_custom_call" | custom-call | flops 200000000 | bytes 1048576 | tf_op jit(solution)/shard_map/radiation_after/pallas_call | solution.py:270
  14.5 0.0 collective-permute-done
  14.5 0.0 collective-permute-done.1
  14.5 0.0 collective-permute-done.2
  14.5 0.0 collective-permute-done.3
  14.5 0.0 copy-start
  14.6 0.7 %copy-done = f32[4,8,128]{2,1,0:T(8,128)S(1)} copy-done((f32[4,8,128]{2,1,0:T(8,128)S(1)}, f32[4,8,128]{2,1,0:T(8,128)}, u32[]{:S(2)}) %copy-start) | copy-done | bytes 16408
  15.2 0.6 %multiply_add_fusion = f32[4,8,128]{2,1,0:T(8,128)} fusion(f32[4,8,128]{2,1,0:T(8,128)S(1)} %copy-done, f32[4,1,128]{2,1,0:T(1,128)S(1)} %get-tuple-element.21, f32[4,1,128]{2,1,0:T(1,128)S(1)} %get-tuple-element.20, f32[1,8,128]{2,1,0:T(8,128)S(1)} %get-tuple-element.19, f32[1,8,128]{2,1,0:T(8,128)S(1)} %get-tuple-element.18), kind=kLoop, calls=%fused_computation | loop fusion | flops 20480 | bytes 45056 | tf_op jit(solution)/shard_map/add | solution.py:289
  (2 shorter events, 0.0 us)
Async XLA Ops:
  0.6 3.8 %copy-start.1 = (f32[4,8,128]{2,1,0:T(8,128)S(1)}, f32[4,8,128]{2,1,0:T(8,128)}, u32[]{:S(2)}) copy-start(f32[4,8,128]{2,1,0:T(8,128)} %temp_ref.1) | copy-start | bytes 49156
  4.5 10.0 %collective-permute-start = (f32[4,8,128]{2,1,0:T(8,128)S(1)}, f32[4,8,128]{2,1,0:T(8,128)S(1)}, u32[]{:S(2)}, u32[]{:S(2)}) collective-permute-start(f32[4,8,128]{2,1,0:T(8,128)S(1)} %copy-done.1), channel_id=1, source_target_pairs={{0,1},{1,0},{2,3},{3,2},{4,5},{5,4},{6,7},{7,6},{8,9},{9,8},{10,11... | collective-permute-start | bytes 49160 | tf_op jit(solution)/shard_map/ppermute | solution.py:267
  6.0 8.5 %collective-permute-start.1 = (f32[4,8,128]{2,1,0:T(8,128)S(1)}, f32[4,8,128]{2,1,0:T(8,128)S(1)}, u32[]{:S(2)}, u32[]{:S(2)}) collective-permute-start(f32[4,8,128]{2,1,0:T(8,128)S(1)} %copy-done.1), channel_id=1, source_target_pairs={{0,120},{8,16},{16,8},{24,32},{32,24},{40,48},{48,40},{56,64},{64,... | collective-permute-start | bytes 49160 | tf_op jit(solution)/shard_map/ppermute | solution.py:267
  7.8 6.7 %collective-permute-start.2 = (f32[4,8,128]{2,1,0:T(8,128)S(1)}, f32[4,8,128]{2,1,0:T(8,128)S(1)}, u32[]{:S(2)}, u32[]{:S(2)}) collective-permute-start(f32[4,8,128]{2,1,0:T(8,128)S(1)} %copy-done.1), channel_id=1, source_target_pairs={{0,8},{8,0},{16,24},{24,16},{32,40},{40,32},{48,56},{56,48},{64,72... | collective-permute-start | bytes 49160 | tf_op jit(solution)/shard_map/ppermute | solution.py:267
  8.5 6.0 %collective-permute-start.3 = (f32[4,8,128]{2,1,0:T(8,128)S(1)}, f32[4,8,128]{2,1,0:T(8,128)S(1)}, u32[]{:S(2)}, u32[]{:S(2)}) collective-permute-start(f32[4,8,128]{2,1,0:T(8,128)S(1)} %copy-done.1), channel_id=1, source_target_pairs={{0,7},{1,2},{2,1},{3,4},{4,3},{5,6},{6,5},{7,0},{8,15},{9,10},{10,... | collective-permute-start | bytes 49160 | tf_op jit(solution)/shard_map/ppermute | solution.py:267
  14.5 0.7 %copy-start = (f32[4,8,128]{2,1,0:T(8,128)S(1)}, f32[4,8,128]{2,1,0:T(8,128)}, u32[]{:S(2)}) copy-start(f32[4,8,128]{2,1,0:T(8,128)} %get-tuple-element.12) | copy-start | bytes 49156
